TPU v7x, 32 devices: a whole 2x2x4 slice. The times are simulated.
32 devices in a mesh: tm: 8 (over z, x), mode: 4 (over y, core).
Axes of the slice: x: 2, y: 2, z: 4, core: 2. Of those that a mesh axis runs over, the one named last changes fastest.
Arguments:
- observations: bfloat16 [512, 2048], P('tm', 'mode'), may hold values from -6 to 6
- basis: bfloat16 [2048, 2048], P(None, 'mode'), may hold values from -0.125 to 0.125
- eigvals: float32 [2048], P('mode'), may hold values from 0.05 to 4
- lengths: float32 [2048], P('mode'), may hold values from 8 to 2048
- noise: float32 [1], replicated, may hold values from 0.3 to 1
Outputs:
- grad_obs: float32 [512, 2048], P('tm', 'mode')
All inputs are finite; a program needn't handle non-finite values.
Results may differ from a plain program's by a relative error of at most 0.0024.
Values may be sent and summed in bfloat16 or wider, within the bound.
No kernel may reach another device: no remote copies, remote signals or barrier semaphores. Data moves between devices by JAX's collectives and lax.ppermute only.
A program may use at most 64 MiB of HBM per device.

v0:
```python
import functools
import math

import jax
import jax.numpy as jnp
from jax import lax
from jax.experimental import pallas as pl
from jax.experimental.pallas import tpu as pltpu
from jax.sharding import PartitionSpec as P

F32 = jnp.float32
SUB = 8
VMEM_LIMIT = 24 * 1024 * 1024


def mat_mul(p, q):
    return (
        p[0] * q[0] + p[1] * q[2],
        p[0] * q[1] + p[1] * q[3],
        p[2] * q[0] + p[3] * q[2],
        p[2] * q[1] + p[3] * q[3],
    )


def mat_trans(p):
    return (p[0], p[2], p[1], p[3])


def mat_add(p, q):
    return tuple(a + b for a, b in zip(p, q))


def mat_sub(p, q):
    return tuple(a - b for a, b in zip(p, q))


def mat_pick(flag, p, q):
    return tuple(jnp.where(flag, a, b) for a, b in zip(p, q))


def full(s):
    return (s[0], s[1], s[1], s[2])


def congruence(s, f):
    t = (
        s[0] * f[0] + s[1] * f[2],
        s[0] * f[1] + s[1] * f[3],
        s[1] * f[0] + s[2] * f[2],
        s[1] * f[1] + s[2] * f[3],
    )
    return (f[0] * t[0] + f[2] * t[2], f[0] * t[1] + f[2] * t[3], f[1] * t[1] + f[3] * t[3])


def power(squares, exponent, like):
    one, zero = jnp.ones_like(like), jnp.zeros_like(like)
    out = None
    for bit, base in enumerate(squares):
        flag = (exponent & (1 << bit)) != 0
        if out is None:
            out = mat_pick(flag, base, (one, zero, zero, one))
        else:
            out = mat_pick(flag, mat_mul(out, base), out)
    return out


def gramian(squares, grams, count, like):
    zero = jnp.zeros_like(like)
    out = (zero, zero, zero)
    for bit, (base, gram) in enumerate(zip(squares, grams)):
        flag = (count & (1 << bit)) != 0
        out = mat_pick(flag, mat_add(gram, congruence(out, base)), out)
    return out


def steady_state(scale2, length, noise_var):
    lam = math.sqrt(3.0) / length
    decay = jnp.exp(-lam)
    twice = 2.0 * lam
    fall = jnp.exp(-twice)
    rho = scale2 / noise_var
    series = 1.0 / 604800.0
    for factor in (60480.0, 6720.0, 840.0, 120.0, 20.0, 4.0, 1.0):
        series = series * twice + 1.0 / factor
    lower = fall * twice * twice * twice * (1.0 / 6.0) * series
    loss = 1.0
    for order in (8, 7, 6, 5, 4, 3, 2):
        loss = 1.0 - lam * (1.0 / order) * loss
    loss = lam * loss
    q00 = rho * lower
    q01 = 2.0 * rho * lam * lam * fall
    q11 = rho * (lower + twice * fall)
    slope = decay * lam
    tilt = loss + slope
    g0 = q00 * tilt * tilt + 2.0 * slope * q01 * tilt + slope * slope * q11
    g1 = slope * q01 - decay * (1.0 - lam) * q00
    loss2 = loss * loss
    c2 = decay * decay
    u = (2.0 * decay * loss2 - g1) / c2
    v = (loss2 * loss2 + g0) / c2
    root = jnp.sqrt(v * (v + 4.0 * u + 16.0))
    product = 4.0 * v / (v + root + jnp.sqrt(2.0 * v * (v + 2.0 * u + root)))
    total = 0.5 * (jnp.sqrt(u * u + 4.0 * u - 2.0 * v + 2.0 * root) - u)
    gain0 = total - 2.0 * loss
    gain1 = (product - loss2 - gain0 * tilt) / slope
    inverse = (1.0 - total + product) / c2
    inn = c2 / (1.0 - total + product)
    closed = (1.0 + slope - loss - gain0, slope, -slope - gain1, decay * (1.0 - lam))
    p00 = inn * ((1.0 - lam) * gain0 - lam * gain1) / decay
    p01 = inn * (lam * gain0 + (1.0 + lam) * gain1) / decay
    p11 = (
        p01 * (loss * (1.0 + decay) + 2.0 * slope * slope)
        + slope * decay * (1.0 + lam) * p00
        - q01
        + gain0 * gain1 * inn
    ) / (slope * decay * (1.0 - lam))
    return closed, gain0, gain1, inverse, (rho - p00, -p01, rho - p11)


def coefficients_kernel(blocks, me_ref, *refs):
    arguments, (const_ref, w_ref, g_ref, basis_ref, obs_ref) = refs[:5], refs[5:10]
    noise_ref, scale_ref, length_ref, sems = refs[10:]
    copies = [
        pltpu.make_async_copy(source, target, sems.at[k])
        for k, (source, target) in enumerate(
            zip(arguments, (noise_ref, scale_ref, length_ref, obs_ref, basis_ref))
        )
    ]
    for copy in copies:
        copy.start()
    for copy in copies[:3]:
        copy.wait()
    steps = w_ref.shape[1]
    width = scale_ref.shape[1]
    tile = (SUB, width)
    me = me_ref[0]
    scale2 = jnp.broadcast_to(scale_ref[...], tile)
    length = jnp.broadcast_to(length_ref[...], tile)
    noise_var = jnp.full(tile, noise_ref[0], F32)
    closed, gain0, gain1, inverse, excess = steady_state(scale2, length, noise_var)
    zero = jnp.zeros(tile, F32)

    squares, grams = [closed], [(inverse, zero, zero)]
    doublings = (steps * blocks).bit_length() - 1
    for _ in range(doublings):
        base = squares[-1]
        grams.append(mat_add(grams[-1], congruence(grams[-1], base)))
        squares.append(mat_mul(base, base))
    local = steps.bit_length() - 1
    consts = closed + (gain0, gain1, inverse) + squares[3] + squares[4] + squares[5]
    for place, value in enumerate(consts):
        const_ref[place] = value
    const_ref[len(consts)] = -1.0 / noise_var

    row = lax.broadcasted_iota(jnp.int32, tile, 0)
    small, gram_small = squares[:3], grams[:3]
    behind = power(small, 7 - row, zero)
    gram = gramian(small, gram_small, 7 - row, zero)
    eight, gram_eight = squares[3], grams[3]
    parts = steps // SUB
    for part in range(parts - 1, -1, -1):
        rows = pl.ds(part * SUB, SUB)
        w_ref[0, rows, :] = behind[0] * gain0 + behind[1] * gain1
        w_ref[1, rows, :] = behind[2] * gain0 + behind[3] * gain1
        k0 = gain0 * gram[0] + gain1 * gram[1]
        k1 = gain0 * gram[1] + gain1 * gram[2]
        w_ref[2, rows, :] = inverse - (k0 * closed[0] + k1 * closed[2])
        w_ref[3, rows, :] = -(k0 * closed[1] + k1 * closed[3])
        if part:
            behind = mat_mul(behind, eight)
            gram = mat_add(gram_eight, congruence(gram, eight))
    ahead = power(small, row, zero)
    for part in range(parts):
        rows = pl.ds(part * SUB, SUB)
        u0, u1 = w_ref[2, rows, :], w_ref[3, rows, :]
        w_ref[2, rows, :] = u0 * ahead[0] + u1 * ahead[2]
        w_ref[3, rows, :] = u0 * ahead[1] + u1 * ahead[3]
        if part < parts - 1:
            ahead = mat_mul(ahead, eight)

    s = grams[-1]
    left = (
        1.0 + excess[0] * s[0] + excess[1] * s[1],
        excess[0] * s[1] + excess[1] * s[2],
        excess[1] * s[0] + excess[2] * s[1],
        1.0 + excess[1] * s[1] + excess[2] * s[2],
    )
    determ = 1.0 / (left[0] * left[3] - left[1] * left[2])
    start = mat_mul((left[3], -left[1], -left[2], left[0]), full(excess))
    start = tuple(x * determ for x in start)
    block_squares, block_grams = squares[local:-1], grams[local:-1]
    mine = jnp.full(tile, me, jnp.int32)
    to_me = power(block_squares, mine, zero)
    rest = full(gramian(block_squares, block_grams, blocks - 1 - mine, zero))
    to_state = mat_mul(to_me, start)
    to_adjoint = mat_mul(mat_mul(rest, mat_mul(to_me, block_squares[0])), start)
    for group in range(4 * blocks // SUB):
        rows = row + group * SUB
        kind = rows & 3
        other = rows >> 2
        gap = jnp.abs(other - me)
        near = power(block_squares, jnp.maximum(gap - 1, 0), zero)
        same = other == me
        one = jnp.ones_like(zero)
        far = mat_pick(same, (one, zero, zero, one), mat_mul(near, block_squares[0]))
        origin = mat_trans(power(block_squares, other, zero))
        left_over = full(gramian(block_squares, block_grams, blocks - 1 - other, zero))
        first = mat_mul(mat_mul(origin, mat_trans(block_squares[0])), left_over)
        before = other < me
        after = other > me
        state_b = mat_sub(mat_pick(before, near, (zero,) * 4), mat_mul(to_state, first))
        state_l = mat_mul(to_state, origin)
        cross = mat_pick(after, mat_mul(mat_trans(far), left_over), mat_mul(rest, far))
        adjoint_b = mat_sub(mat_mul(to_adjoint, first), cross)
        adjoint_l = mat_sub(
            mat_pick(after, mat_trans(near), (zero,) * 4), mat_mul(to_adjoint, origin)
        )
        place = pl.ds(group * SUB, SUB)
        for line, (from_b, from_l) in enumerate(
            ((adjoint_b[:2], adjoint_l[:2]), (adjoint_b[2:], adjoint_l[2:]),
             (state_b[:2], state_l[:2]), (state_b[2:], state_l[2:]))
        ):
            g_ref[line, place, :] = jnp.where(
                kind < 2,
                jnp.where(kind == 0, from_b[0], from_b[1]),
                jnp.where(kind == 2, from_l[0], from_l[1]),
            )
    for copy in copies[3:]:
        copy.wait()


def rotate_kernel(pieces, place_ref, *refs):
    obs_refs = refs[:pieces]
    basis_ref, w_ref, z_ref, sum_ref = refs[pieces:]
    depth = obs_refs[0].shape[1]
    z = None
    for piece, obs_ref in enumerate(obs_refs):
        begin = pl.multiple_of((place_ref[0] ^ piece) * depth, depth)
        term = jnp.dot(
            obs_ref[...], basis_ref[pl.ds(begin, depth), :], preferred_element_type=F32
        )
        z = term if z is None else z + term
    z_ref[...] = z
    for line in range(4):
        summary = jnp.sum(w_ref[line] * z, axis=0, keepdims=True)
        for block in range(sum_ref.shape[0]):
            sum_ref[block, line : line + 1, :] = summary


def shift(value, by):
    rows = value.shape[0]
    row = lax.broadcasted_iota(jnp.int32, value.shape, 0)
    keep = row >= by if by > 0 else row < rows + by
    return jnp.where(keep, pltpu.roll(value, by % rows, 0), 0.0)


def local_kernel(z_ref, const_ref, r_ref, scratch):
    steps, width = z_ref.shape
    span = steps // SUB
    lanes = 128
    for chunk in range(width // lanes):
        cols = pl.ds(chunk * lanes, lanes)
        scratch[chunk] = z_ref[:, cols]
    for chunk in range(width // lanes):
        cols = pl.ds(chunk * lanes, lanes)
        const = [const_ref[k, :, cols] for k in range(19)]
        f, (k0, k1, inverse) = const[0:4], const[4:7]
        jumps = (const[7:11], const[11:15], const[15:19])
        zero = jnp.zeros((SUB, lanes), F32)
        x0, x1 = zero, zero
        vs = []
        for t in range(span):
            z = scratch[chunk, pl.ds(t, SUB, stride=span), :]
            vs.append(z - x0)
            x0, x1 = f[0] * x0 + f[1] * x1 + k0 * z, f[2] * x0 + f[3] * x1 + k1 * z
        for level, jump in enumerate(jumps):
            s0, s1 = shift(x0, 1 << level), shift(x1, 1 << level)
            x0, x1 = x0 + jump[0] * s0 + jump[1] * s1, x1 + jump[2] * s0 + jump[3] * s1
        x0, x1 = shift(x0, 1), shift(x1, 1)
        for t in range(span):
            vs[t] = (vs[t] - x0) * inverse
            x0, x1 = f[0] * x0 + f[1] * x1, f[2] * x0 + f[3] * x1
        a0, a1 = zero, zero
        for t in range(span - 1, -1, -1):
            a0, a1 = f[0] * a0 + f[2] * a1 + vs[t], f[1] * a0 + f[3] * a1
        for level, jump in enumerate(jumps):
            s0, s1 = shift(a0, -(1 << level)), shift(a1, -(1 << level))
            a0, a1 = a0 + jump[0] * s0 + jump[2] * s1, a1 + jump[1] * s0 + jump[3] * s1
        a0, a1 = shift(a0, -1), shift(a1, -1)
        for t in range(span - 1, -1, -1):
            r = vs[t] - k0 * a0 - k1 * a1
            a0, a1 = f[0] * a0 + f[2] * a1 + vs[t], f[1] * a0 + f[3] * a1
            scratch[chunk, pl.ds(t, SUB, stride=span), :] = r
        r_ref[:, cols] = scratch[chunk]


def finish_kernel(place_ref, r_ref, w_ref, g_ref, const_ref, basis_ref, sums_ref, *outs):
    blocks, pieces = sums_ref.shape[0], len(outs)
    depth = outs[0].shape[1]
    value = r_ref[...]
    for line in range(4):
        total = None
        for block in range(blocks):
            term = g_ref[line, pl.ds(4 * block, 4), :] * sums_ref[block]
            total = term if total is None else total + term
        value = value - w_ref[line] * jnp.sum(total, axis=0, keepdims=True)
    scale = const_ref[19, 0:1, :]
    residual = (value * scale).astype(jnp.bfloat16)
    for piece in range(pieces - 1, -1, -1):
        begin = pl.multiple_of((place_ref[0] ^ piece) * depth, depth)
        outs[piece][...] = lax.dot_general(
            residual,
            basis_ref[pl.ds(begin, depth), :],
            (((1,), (1,)), ((), ())),
            preferred_element_type=F32,
        ).astype(outs[piece].dtype)


def exchange(value, axis, count):
    out = [value]
    for step in range(1, count):
        out.append(lax.ppermute(value, axis, [(a, a ^ step) for a in range(count)]))
    return out


def shards(observations, basis, eigvals, lengths, noise):
    steps, depth = observations.shape
    width = basis.shape[1]
    blocks, pieces = lax.axis_size("tm"), lax.axis_size("mode")
    me = lax.axis_index("tm").astype(jnp.int32).reshape(1)
    place = lax.axis_index("mode").astype(jnp.int32).reshape(1)
    vmem = pl.BlockSpec(memory_space=pltpu.VMEM)
    smem = pl.BlockSpec(memory_space=pltpu.SMEM)
    params = pltpu.CompilerParams(vmem_limit_bytes=VMEM_LIMIT)

    def shape(*dims, dtype=F32):
        return jax.ShapeDtypeStruct(dims, dtype)

    obs = exchange(observations, "mode", pieces)
    const, w, g, basis, obs[0] = pl.pallas_call(
        functools.partial(coefficients_kernel, blocks),
        out_shape=(
            shape(20, SUB, width),
            shape(4, steps, width),
            shape(4, 4 * blocks, width),
            shape(*basis.shape, dtype=basis.dtype),
            shape(steps, depth, dtype=observations.dtype),
        ),
        in_specs=[smem] + [pl.BlockSpec(memory_space=pltpu.HBM)] * 5,
        out_specs=(vmem,) * 5,
        scratch_shapes=[
            pltpu.SMEM((1,), F32),
            pltpu.VMEM((1, width), F32),
            pltpu.VMEM((1, width), F32),
            pltpu.SemaphoreType.DMA((5,)),
        ],
        compiler_params=params,
        cost_estimate=pl.CostEstimate(flops=20000000, bytes_accessed=2000000, transcendentals=0),
        name="coefficients",
    )(me, noise, eigvals.reshape(1, width), lengths.reshape(1, width), observations, basis)
    z, summary = pl.pallas_call(
        functools.partial(rotate_kernel, pieces),
        out_shape=(shape(steps, width), shape(blocks, 4, width)),
        in_specs=[smem] + [vmem] * (pieces + 2),
        out_specs=(vmem,) * 2,
        compiler_params=params,
        name="rotate",
    )(place, *obs, basis, w)
    sums = lax.all_to_all(summary, "tm", 0, 0)
    local = pl.pallas_call(
        local_kernel,
        out_shape=shape(steps, width),
        in_specs=[vmem] * 2,
        out_specs=vmem,
        scratch_shapes=[pltpu.VMEM((width // 128, steps, 128), F32)],
        compiler_params=params,
        cost_estimate=pl.CostEstimate(flops=10000000, bytes_accessed=1000000, transcendentals=0),
        name="local",
    )(z, const)
    parts = pl.pallas_call(
        finish_kernel,
        out_shape=(shape(steps, depth),)
        + (shape(steps, depth, dtype=jnp.bfloat16),) * (pieces - 1),
        in_specs=[smem] + [vmem] * 6,
        out_specs=(vmem,) * pieces,
        compiler_params=params,
        name="finish",
    )(place, local, w, g, const, basis, sums)
    grad_obs = parts[0]
    for step in range(1, pieces):
        grad_obs = grad_obs + lax.ppermute(
            parts[step], "mode", [(a, a ^ step) for a in range(pieces)]
        ).astype(F32)
    return grad_obs


def solution(mesh):
    placed = (P("tm", "mode"), P(None, "mode"), P("mode"), P("mode"), P())
    return jax.shard_map(
        shards, mesh=mesh, in_specs=placed, out_specs=P("tm", "mode"), check_vma=False
    )
```

profile of v0, /device:TPU:0, one launch (start us, length us, event | category | flops | bytes accessed | tf_op | source)
XLA Modules:
  0.0 31.1 jit_solution(15520684189090774610)
XLA Ops:
  0.0 0.5 %collective-permute-start = (bf16[64,512]{1,0:T(8,128)(2,1)}, bf16[64,512]{1,0:T(8,128)(2,1)S(1)}, u32[]{:S(2)}, u32[]{:S(2)}) collective-permute-start(bf16[64,512]{1,0:T(8,128)(2,1)} %refs_3_.1), channel_id=1, source_target_pairs={{0,1},{1,0},{2,3},{3,2},{4,5},{5,4},{6,7},{7,6},{8,9},{9,8},{10,11... | collective-permute-start | bytes 196616 | tf_op jit(solution)/shard_map/ppermute | solution.py:322
  0.5 2.6 %collective-permute-start.2 = (bf16[64,512]{1,0:T(8,128)(2,1)}, bf16[64,512]{1,0:T(8,128)(2,1)S(1)}, u32[]{:S(2)}, u32[]{:S(2)}) collective-permute-start(bf16[64,512]{1,0:T(8,128)(2,1)} %refs_3_.1), channel_id=1, source_target_pairs={{0,3},{1,2},{2,1},{3,0},{4,7},{5,6},{6,5},{7,4},{8,11},{9,10},{10,... | collective-permute-start | bytes 196616 | tf_op jit(solution)/shard_map/ppermute | solution.py:322
  3.1 0.0 collective-permute-start.1
  3.7 0.0 copy-start
  3.7 1.6 %copy-done = bf16[2048,512]{1,0:T(8,128)(2,1)S(1)} copy-done((bf16[2048,512]{1,0:T(8,128)(2,1)S(1)}, bf16[2048,512]{1,0:T(8,128)(2,1)}, u32[]{:S(2)}) %copy-start) | copy-done | bytes 2097176
  5.3 0.0 copy-start.1
  5.3 0.8 %copy-done.1 = bf16[64,512]{1,0:T(8,128)(2,1)S(1)} copy-done((bf16[64,512]{1,0:T(8,128)(2,1)S(1)}, bf16[64,512]{1,0:T(8,128)(2,1)}, u32[]{:S(2)}) %copy-start.1) | copy-done | bytes 65560
  6.2 0.0 copy-start.3
  6.2 0.7 %copy-done.3 = f32[512]{0:T(512)S(1)} copy-done((f32[512]{0:T(512)S(1)}, f32[512]{0:T(512)}, u32[]{:S(2)}) %copy-start.3) | copy-done | bytes 2072
  6.9 0.0 copy-start.4
  6.9 0.7 %copy-done.4 = f32[512]{0:T(512)S(1)} copy-done((f32[512]{0:T(512)S(1)}, f32[512]{0:T(512)}, u32[]{:S(2)}) %copy-start.4) | copy-done | bytes 2072
  7.5 2.0 %coefficients.1 = (f32[20,8,512]{2,1,0:T(8,128)S(1)}, f32[4,64,512]{2,1,0:T(8,128)S(1)}, f32[4,32,512]{2,1,0:T(8,128)S(1)}, bf16[2048,512]{1,0:T(8,128)(2,1)S(1)}, bf16[64,512]{1,0:T(8,128)(2,1)S(1)}) custom-call(s32[1]{0:T(128)} %bitcast.1.me_ref, f32[1]{0:T(128)S(6)} %copy.6.refs_0_, f32[1,512]{1,0:T(1,128)S(1)} %bitcast.4, f32[1,512]{1,0:T(1,128)S(1)} %bitcast.5, ...), custom_call_target="tpu_custom_call" | custom-call | flops 20000000 | bytes 2000000 | tf_op jit(solution)/shard_map/coefficients/pallas_call | solution.py:340
  9.5 0.0 collective-permute-done.refs_1_
  9.6 0.0 collective-permute-done.2.refs_3_
  9.6 0.0 collective-permute-done.1.refs_2_
  9.6 0.5 %rotate.1 = (f32[64,512]{1,0:T(8,128)S(1)}, f32[8,4,512]{2,1,0:T(4,128)S(1)}) custom-call(s32[1]{0:T(128)} %bitcast.place_ref, bf16[64,512]{1,0:T(8,128)(2,1)S(1)} %get-tuple-element.16.refs_0_, bf16[64,512]{1,0:T(8,128)(2,1)S(1)} %collective-permute-done.refs_1_, bf16[64,512]{1,0:T(8,128)(2,1)S(1)} %collective-permute-done.1.refs_2_, ...), custom_call_target="tpu_custom_call" | custom-call | tf_op jit(solution)/shard_map/rotate/pallas_call | solution.py:361
  10.1 0.0 copy-start.2
  10.1 0.6 %copy-done.2 = f32[8,4,512]{2,1,0:T(4,128)} copy-done((f32[8,4,512]{2,1,0:T(4,128)}, f32[8,4,512]{2,1,0:T(4,128)S(1)}, u32[]{:S(2)}) %copy-start.2) | copy-done | bytes 65560
  10.7 6.3 %all-to-all-start = ((f32[8,4,512]{2,1,0:T(4,128)}), f32[8,4,512]{2,1,0:T(4,128)S(1)}, u32[]{:S(2)}, u32[]{:S(2)}) async-start(f32[8,4,512]{2,1,0:T(4,128)} %copy-done.2), calls=%async_computation | async-start | bytes 131072 | tf_op jit(solution)/shard_map/all_to_all | solution.py:369
  17.0 0.3 local.1.r_ref
  17.3 6.6 %all-to-all-done.sums_ref = f32[8,4,512]{2,1,0:T(4,128)S(1)} async-done(((f32[8,4,512]{2,1,0:T(4,128)}), f32[8,4,512]{2,1,0:T(4,128)S(1)}, u32[]{:S(2)}, u32[]{:S(2)}) %all-to-all-start) | async-done | bytes 65568 | tf_op jit(solution)/shard_map/all_to_all | solution.py:369
  24.0 0.7 %finish.1 = (f32[64,512]{1,0:T(8,128)S(1)}, bf16[64,512]{1,0:T(8,128)(2,1)S(1)}, bf16[64,512]{1,0:T(8,128)(2,1)S(1)}, bf16[64,512]{1,0:T(8,128)(2,1)S(1)}) custom-call(s32[1]{0:T(128)} %bitcast.place_ref, f32[64,512]{1,0:T(8,128)S(1)} %local.1.r_ref, f32[4,64,512]{2,1,0:T(8,128)S(1)} %get-tuple-element.18.refs_5_.w_ref, ...), custom_call_target="tpu_custom_call" | custom-call | tf_op jit(solution)/shard_map/finish/pallas_call | solution.py:380
  24.7 0.1 collective-permute-start.3
  24.8 1.6 %collective-permute-start.4 = (bf16[64,512]{1,0:T(8,128)(2,1)S(1)}, bf16[64,512]{1,0:T(8,128)(2,1)S(1)}, u32[]{:S(2)}, u32[]{:S(2)}) collective-permute-start(bf16[64,512]{1,0:T(8,128)(2,1)S(1)} %get-tuple-element.25), channel_id=1, source_target_pairs={{0,2},{1,3},{2,0},{3,1},{4,6},{5,7},{6,4},{7,5},{8,10},{9,11},{10,... | collective-permute-start | bytes 196616 | tf_op jit(solution)/shard_map/ppermute | solution.py:391
  26.4 0.3 collective-permute-start.5
  26.6 0.0 collective-permute-done.3
  26.6 2.6 %collective-permute-done.4 = bf16[64,512]{1,0:T(8,128)(2,1)S(1)} collective-permute-done((bf16[64,512]{1,0:T(8,128)(2,1)S(1)}, bf16[64,512]{1,0:T(8,128)(2,1)S(1)}, u32[]{:S(2)}, u32[]{:S(2)}) %collective-permute-start.4) | collective-permute-done | bytes 65568 | tf_op jit(solution)/shard_map/ppermute | solution.py:391
  29.3 1.1 %collective-permute-done.5 = bf16[64,512]{1,0:T(8,128)(2,1)S(1)} collective-permute-done((bf16[64,512]{1,0:T(8,128)(2,1)S(1)}, bf16[64,512]{1,0:T(8,128)(2,1)S(1)}, u32[]{:S(2)}, u32[]{:S(2)}) %collective-permute-start.5) | collective-permute-done | bytes 65568 | tf_op jit(solution)/shard_map/ppermute | solution.py:391
  30.4 0.7 %convert_add_fusion = f32[64,512]{1,0:T(8,128)} fusion(bf16[64,512]{1,0:T(8,128)(2,1)S(1)} %collective-permute-done.5, bf16[64,512]{1,0:T(8,128)(2,1)S(1)} %collective-permute-done.4, f32[64,512]{1,0:T(8,128)S(1)} %get-tuple-element.23, bf16[64,512]{1,0:T(8,128)(2,1)S(1)} %collective-permute-done.3), kind=kLoop, calls=%fused_computation | loop fusion | flops 196608 | bytes 458752 | tf_op jit(solution)/shard_map/add | solution.py:391
Async XLA Ops:
  0.0 9.5 %collective-permute-start = (bf16[64,512]{1,0:T(8,128)(2,1)}, bf16[64,512]{1,0:T(8,128)(2,1)S(1)}, u32[]{:S(2)}, u32[]{:S(2)}) collective-permute-start(bf16[64,512]{1,0:T(8,128)(2,1)} %refs_3_.1), channel_id=1, source_target_pairs={{0,1},{1,0},{2,3},{3,2},{4,5},{5,4},{6,7},{7,6},{8,9},{9,8},{10,11... | collective-permute-start | bytes 196616 | tf_op jit(solution)/shard_map/ppermute | solution.py:322
  0.5 9.1 %collective-permute-start.2 = (bf16[64,512]{1,0:T(8,128)(2,1)}, bf16[64,512]{1,0:T(8,128)(2,1)S(1)}, u32[]{:S(2)}, u32[]{:S(2)}) collective-permute-start(bf16[64,512]{1,0:T(8,128)(2,1)} %refs_3_.1), channel_id=1, source_target_pairs={{0,3},{1,2},{2,1},{3,0},{4,7},{5,6},{6,5},{7,4},{8,11},{9,10},{10,... | collective-permute-start | bytes 196616 | tf_op jit(solution)/shard_map/ppermute | solution.py:322
  3.1 6.5 %collective-permute-start.1 = (bf16[64,512]{1,0:T(8,128)(2,1)}, bf16[64,512]{1,0:T(8,128)(2,1)S(1)}, u32[]{:S(2)}, u32[]{:S(2)}) collective-permute-start(bf16[64,512]{1,0:T(8,128)(2,1)} %refs_3_.1), channel_id=1, source_target_pairs={{0,2},{1,3},{2,0},{3,1},{4,6},{5,7},{6,4},{7,5},{8,10},{9,11},{10,... | collective-permute-start | bytes 196616 | tf_op jit(solution)/shard_map/ppermute | solution.py:322
  3.7 1.6 %copy-start = (bf16[2048,512]{1,0:T(8,128)(2,1)S(1)}, bf16[2048,512]{1,0:T(8,128)(2,1)}, u32[]{:S(2)}) copy-start(bf16[2048,512]{1,0:T(8,128)(2,1)} %refs_4_.1) | copy-start | bytes 6291460
  5.3 0.8 %copy-start.1 = (bf16[64,512]{1,0:T(8,128)(2,1)S(1)}, bf16[64,512]{1,0:T(8,128)(2,1)}, u32[]{:S(2)}) copy-start(bf16[64,512]{1,0:T(8,128)(2,1)} %refs_3_.1) | copy-start | bytes 196612
  6.2 0.7 %copy-start.3 = (f32[512]{0:T(512)S(1)}, f32[512]{0:T(512)}, u32[]{:S(2)}) copy-start(f32[512]{0:T(512)} %param.7) | copy-start | bytes 6148
  6.9 0.7 %copy-start.4 = (f32[512]{0:T(512)S(1)}, f32[512]{0:T(512)}, u32[]{:S(2)}) copy-start(f32[512]{0:T(512)} %param.8) | copy-start | bytes 6148
  10.1 0.6 %copy-start.2 = (f32[8,4,512]{2,1,0:T(4,128)}, f32[8,4,512]{2,1,0:T(4,128)S(1)}, u32[]{:S(2)}) copy-start(f32[8,4,512]{2,1,0:T(4,128)S(1)} %get-tuple-element.22) | copy-start | bytes 196612
  10.7 13.2 %all-to-all-start = ((f32[8,4,512]{2,1,0:T(4,128)}), f32[8,4,512]{2,1,0:T(4,128)S(1)}, u32[]{:S(2)}, u32[]{:S(2)}) async-start(f32[8,4,512]{2,1,0:T(4,128)} %copy-done.2), calls=%async_computation | async-start | bytes 131072 | tf_op jit(solution)/shard_map/all_to_all | solution.py:369
  24.7 1.9 %collective-permute-start.3 = (bf16[64,512]{1,0:T(8,128)(2,1)S(1)}, bf16[64,512]{1,0:T(8,128)(2,1)S(1)}, u32[]{:S(2)}, u32[]{:S(2)}) collective-permute-start(bf16[64,512]{1,0:T(8,128)(2,1)S(1)} %get-tuple-element.24), channel_id=1, source_target_pairs={{0,1},{1,0},{2,3},{3,2},{4,5},{5,4},{6,7},{7,6},{8,9},{9,8},{10,11... | collective-permute-start | bytes 196616 | tf_op jit(solution)/shard_map/ppermute | solution.py:391
  24.8 4.5 %collective-permute-start.4 = (bf16[64,512]{1,0:T(8,128)(2,1)S(1)}, bf16[64,512]{1,0:T(8,128)(2,1)S(1)}, u32[]{:S(2)}, u32[]{:S(2)}) collective-permute-start(bf16[64,512]{1,0:T(8,128)(2,1)S(1)} %get-tuple-element.25), channel_id=1, source_target_pairs={{0,2},{1,3},{2,0},{3,1},{4,6},{5,7},{6,4},{7,5},{8,10},{9,11},{10,... | collective-permute-start | bytes 196616 | tf_op jit(solution)/shard_map/ppermute | solution.py:391
  26.4 4.0 %collective-permute-start.5 = (bf16[64,512]{1,0:T(8,128)(2,1)S(1)}, bf16[64,512]{1,0:T(8,128)(2,1)S(1)}, u32[]{:S(2)}, u32[]{:S(2)}) collective-permute-start(bf16[64,512]{1,0:T(8,128)(2,1)S(1)} %get-tuple-element.26), channel_id=1, source_target_pairs={{0,3},{1,2},{2,1},{3,0},{4,7},{5,6},{6,5},{7,4},{8,11},{9,10},{10,... | collective-permute-start | bytes 196616 | tf_op jit(solution)/shard_map/ppermute | solution.py:391
where the time goes:
time: 31.4 us; the launch traced here: 31.1 us
  starting transfers between devices  11.3 us (36%)
  waiting for transfers between devices  10.4 us (33%)
  local copies, waits for them, and re-layouts  4.41 us (14%)
  Pallas kernels  3.55 us (11%)
  between operations  0.73 us (2%)
  other arithmetic  0.69 us (2%)
    all_to_all x1, waiting for transfers between devices, shards(): sums = lax.all_to_all(summary, 'tm', 0, 0)  6.63 us
    all_to_all x1, starting transfers between devices, shards(): sums = lax.all_to_all(summary, 'tm', 0, 0)  6.31 us
    unnamed x10, local copies, waits for them, and re-layouts  4.41 us
    ppermute x3, waiting for transfers between devices, shards(): lax.ppermute(parts[step], 'mode', [(a, a ^ step) for a in range(pieces)])  3.77 us
    ppermute x3, starting transfers between devices, exchange(): out.append(lax.ppermute(value, axis, [(a, a ^ step) for a in range(count)]))  3.08 us
    pallas_call x1, Pallas kernels, shards(): pl.pallas_call(functools.partial(coefficients_kernel, blocks), out_shape=...  2 us
    ppermute x3, starting transfers between devices, shards(): lax.ppermute(parts[step], 'mode', [(a, a ^ step) for a in range(pieces)])  1.93 us
    pallas_call x1, Pallas kernels, shards(): pl.pallas_call(finish_kernel, out_shape=(shape(steps, depth),) + (shape(s...  0.75 us
  transfers between devices with their start and end apart: 7, of which 3 were waited for; matrix products, arithmetic and copies ran while one was open for 0% of the time, Pallas kernels for 7%

commit v1 on v0

--- a/solution.py
+++ b/solution.py
@@ -117,18 +117,21 @@
     return closed, gain0, gain1, inverse, (rho - p00, -p01, rho - p11)
 
 
-def coefficients_kernel(blocks, me_ref, *refs):
-    arguments, (const_ref, w_ref, g_ref, basis_ref, obs_ref) = refs[:5], refs[5:10]
-    noise_ref, scale_ref, length_ref, sems = refs[10:]
+def coefficients_kernel(blocks, me_ref, noise_ref, *refs):
+    arguments, (const_ref, w_ref, g_ref, merge_ref, basis_ref, obs_ref) = (
+        refs[:4],
+        refs[4:10],
+    )
+    scale_ref, length_ref, sems = refs[10:]
     copies = [
         pltpu.make_async_copy(source, target, sems.at[k])
         for k, (source, target) in enumerate(
-            zip(arguments, (noise_ref, scale_ref, length_ref, obs_ref, basis_ref))
+            zip(arguments, (scale_ref, length_ref, obs_ref, basis_ref))
         )
     ]
     for copy in copies:
         copy.start()
-    for copy in copies[:3]:
+    for copy in copies[:2]:
         copy.wait()
     steps = w_ref.shape[1]
     width = scale_ref.shape[1]
@@ -151,6 +154,9 @@
     for place, value in enumerate(consts):
         const_ref[place] = value
     const_ref[len(consts)] = -1.0 / noise_var
+    for level in range(blocks.bit_length() - 1):
+        for place, value in enumerate(squares[local + level] + grams[local + level]):
+            merge_ref[7 * level + place : 7 * level + place + 1, :] = value[0:1, :]
 
     row = lax.broadcasted_iota(jnp.int32, tile, 0)
     small, gram_small = squares[:3], grams[:3]
@@ -194,20 +200,23 @@
     rest = full(gramian(block_squares, block_grams, blocks - 1 - mine, zero))
     to_state = mat_mul(to_me, start)
     to_adjoint = mat_mul(mat_mul(rest, mat_mul(to_me, block_squares[0])), start)
-    for group in range(4 * blocks // SUB):
+    for group in range(g_ref.shape[1] // SUB):
         rows = row + group * SUB
         kind = rows & 3
-        other = rows >> 2
-        gap = jnp.abs(other - me)
-        near = power(block_squares, jnp.maximum(gap - 1, 0), zero)
-        same = other == me
-        one = jnp.ones_like(zero)
-        far = mat_pick(same, (one, zero, zero, one), mat_mul(near, block_squares[0]))
-        origin = mat_trans(power(block_squares, other, zero))
-        left_over = full(gramian(block_squares, block_grams, blocks - 1 - other, zero))
-        first = mat_mul(mat_mul(origin, mat_trans(block_squares[0])), left_over)
-        before = other < me
-        after = other > me
+        line = rows >> 2
+        span = jnp.where(line == 0, 1, jnp.left_shift(1, jnp.maximum(line - 1, 0)))
+        near_me = jnp.where(line == 0, mine, mine ^ span)
+        front = jnp.minimum((near_me // span) * span, blocks - 1)
+        back = jnp.minimum(front + span - 1, blocks - 1)
+        before, after = back < me, front > me
+        gap = jnp.where(before, me - 1 - back, jnp.where(after, front - 1 - me, 0))
+        reach = jnp.where(before, me - back, jnp.where(after, back - me, 0))
+        near = power(block_squares, gap, zero)
+        far = power(block_squares, reach, zero)
+        origin = mat_trans(power(block_squares, front, zero))
+        left_over = full(gramian(block_squares, block_grams, blocks - 1 - back, zero))
+        end = mat_trans(mat_mul(power(block_squares, back, zero), block_squares[0]))
+        first = mat_mul(end, left_over)
         state_b = mat_sub(mat_pick(before, near, (zero,) * 4), mat_mul(to_state, first))
         state_l = mat_mul(to_state, origin)
         cross = mat_pick(after, mat_mul(mat_trans(far), left_over), mat_mul(rest, far))
@@ -216,16 +225,16 @@
             mat_pick(after, mat_trans(near), (zero,) * 4), mat_mul(to_adjoint, origin)
         )
         place = pl.ds(group * SUB, SUB)
-        for line, (from_b, from_l) in enumerate(
+        for output, (from_b, from_l) in enumerate(
             ((adjoint_b[:2], adjoint_l[:2]), (adjoint_b[2:], adjoint_l[2:]),
              (state_b[:2], state_l[:2]), (state_b[2:], state_l[2:]))
         ):
-            g_ref[line, place, :] = jnp.where(
+            g_ref[output, place, :] = jnp.where(
                 kind < 2,
                 jnp.where(kind == 0, from_b[0], from_b[1]),
                 jnp.where(kind == 2, from_l[0], from_l[1]),
             )
-    for copy in copies[3:]:
+    for copy in copies[2:]:
         copy.wait()
 
 
@@ -242,9 +251,23 @@
         z = term if z is None else z + term
     z_ref[...] = z
     for line in range(4):
-        summary = jnp.sum(w_ref[line] * z, axis=0, keepdims=True)
-        for block in range(sum_ref.shape[0]):
-            sum_ref[block, line : line + 1, :] = summary
+        sum_ref[line : line + 1, :] = jnp.sum(w_ref[line] * z, axis=0, keepdims=True)
+
+
+def merge_kernel(level, me_ref, own_ref, other_ref, merge_ref, out_ref):
+    own, other = own_ref[...], other_ref[...]
+    lower = jnp.full(own.shape, (me_ref[0] >> level) & 1, jnp.int32) == 0
+    left, right = jnp.where(lower, own, other), jnp.where(lower, other, own)
+    f00, f01, f10, f11, s00, s01, s11 = (
+        merge_ref[7 * level + k : 7 * level + k + 1, :] for k in range(7)
+    )
+    b0, b1 = left[0:1, :], left[1:2, :]
+    a0 = right[2:3, :] - s00 * b0 - s01 * b1
+    a1 = right[3:4, :] - s01 * b0 - s11 * b1
+    out_ref[0:1, :] = right[0:1, :] + f00 * b0 + f01 * b1
+    out_ref[1:2, :] = right[1:2, :] + f10 * b0 + f11 * b1
+    out_ref[2:3, :] = left[2:3, :] + f00 * a0 + f10 * a1
+    out_ref[3:4, :] = left[3:4, :] + f01 * a0 + f11 * a1
 
 
 def shift(value, by):
@@ -294,14 +317,14 @@
         r_ref[:, cols] = scratch[chunk]
 
 
-def finish_kernel(place_ref, r_ref, w_ref, g_ref, const_ref, basis_ref, sums_ref, *outs):
-    blocks, pieces = sums_ref.shape[0], len(outs)
+def finish_kernel(pieces, place_ref, r_ref, w_ref, g_ref, const_ref, basis_ref, *refs):
+    sums, outs = refs[:-pieces], refs[-pieces:]
     depth = outs[0].shape[1]
     value = r_ref[...]
     for line in range(4):
         total = None
-        for block in range(blocks):
-            term = g_ref[line, pl.ds(4 * block, 4), :] * sums_ref[block]
+        for place, sum_ref in enumerate(sums):
+            term = g_ref[line, pl.ds(4 * place, 4), :] * sum_ref[...]
             total = term if total is None else total + term
         value = value - w_ref[line] * jnp.sum(total, axis=0, keepdims=True)
     scale = const_ref[19, 0:1, :]
@@ -329,6 +352,7 @@
     blocks, pieces = lax.axis_size("tm"), lax.axis_size("mode")
     me = lax.axis_index("tm").astype(jnp.int32).reshape(1)
     place = lax.axis_index("mode").astype(jnp.int32).reshape(1)
+    rounds = blocks.bit_length() - 1
     vmem = pl.BlockSpec(memory_space=pltpu.VMEM)
     smem = pl.BlockSpec(memory_space=pltpu.SMEM)
     params = pltpu.CompilerParams(vmem_limit_bytes=VMEM_LIMIT)
@@ -337,36 +361,61 @@
         return jax.ShapeDtypeStruct(dims, dtype)
 
     obs = exchange(observations, "mode", pieces)
-    const, w, g, basis, obs[0] = pl.pallas_call(
+    const, w, g, merge, basis, obs[0] = pl.pallas_call(
         functools.partial(coefficients_kernel, blocks),
         out_shape=(
             shape(20, SUB, width),
             shape(4, steps, width),
-            shape(4, 4 * blocks, width),
+            shape(4, -(-4 * (rounds + 1) // SUB) * SUB, width),
+            shape(-(-7 * rounds // SUB) * SUB, width),
             shape(*basis.shape, dtype=basis.dtype),
             shape(steps, depth, dtype=observations.dtype),
         ),
-        in_specs=[smem] + [pl.BlockSpec(memory_space=pltpu.HBM)] * 5,
-        out_specs=(vmem,) * 5,
+        in_specs=[smem] * 2 + [pl.BlockSpec(memory_space=pltpu.HBM)] * 4,
+        out_specs=(vmem,) * 6,
         scratch_shapes=[
-            pltpu.SMEM((1,), F32),
             pltpu.VMEM((1, width), F32),
             pltpu.VMEM((1, width), F32),
-            pltpu.SemaphoreType.DMA((5,)),
+            pltpu.SemaphoreType.DMA((4,)),
         ],
         compiler_params=params,
         cost_estimate=pl.CostEstimate(flops=20000000, bytes_accessed=2000000, transcendentals=0),
         name="coefficients",
-    )(me, noise, eigvals.reshape(1, width), lengths.reshape(1, width), observations, basis)
+    )(
+        me,
+        noise,
+        *(
+            pltpu.with_memory_space_constraint(x, pltpu.HBM)
+            for x in (
+                eigvals.reshape(1, width),
+                lengths.reshape(1, width),
+                observations,
+                basis,
+            )
+        ),
+    )
     z, summary = pl.pallas_call(
         functools.partial(rotate_kernel, pieces),
-        out_shape=(shape(steps, width), shape(blocks, 4, width)),
+        out_shape=(shape(steps, width), shape(4, width)),
         in_specs=[smem] + [vmem] * (pieces + 2),
         out_specs=(vmem,) * 2,
         compiler_params=params,
         name="rotate",
     )(place, *obs, basis, w)
-    sums = lax.all_to_all(summary, "tm", 0, 0)
+    sums = [summary]
+    for level in range(rounds):
+        step = 1 << level
+        other = lax.ppermute(summary, "tm", [(a, a ^ step) for a in range(blocks)])
+        sums.append(other)
+        if level < rounds - 1:
+            summary = pl.pallas_call(
+                functools.partial(merge_kernel, level),
+                out_shape=shape(4, width),
+                in_specs=[smem] + [vmem] * 3,
+                out_specs=vmem,
+                compiler_params=params,
+                name="merge",
+            )(me, summary, other, merge)
     local = pl.pallas_call(
         local_kernel,
         out_shape=shape(steps, width),
@@ -378,14 +427,14 @@
         name="local",
     )(z, const)
     parts = pl.pallas_call(
-        finish_kernel,
+        functools.partial(finish_kernel, pieces),
         out_shape=(shape(steps, depth),)
         + (shape(steps, depth, dtype=jnp.bfloat16),) * (pieces - 1),
-        in_specs=[smem] + [vmem] * 6,
+        in_specs=[smem] + [vmem] * (5 + len(sums)),
         out_specs=(vmem,) * pieces,
         compiler_params=params,
         name="finish",
-    )(place, local, w, g, const, basis, sums)
+    )(place, local, w, g, const, basis, *sums)
     grad_obs = parts[0]
     for step in range(1, pieces):
         grad_obs = grad_obs + lax.ppermute(

time: 31.4 us -> 27.5 us (0.88)
  local copies, waits for them, and re-layouts: 4.41 us -> 0 us
  waiting for transfers between devices: 10.4 us -> 11.3 us
  starting transfers between devices: 11.3 us -> 10.9 us
    all_to_all x1 -> x0, waiting for transfers between devices: 6.63 us -> none  [shards(): sums = lax.all_to_all(summary, 'tm', 0, 0)]
    all_to_all x1 -> x0, starting transfers between devices: 6.31 us -> none  [shards(): sums = lax.all_to_all(summary, 'tm', 0, 0)]
    ppermute x0 -> x3, waiting for transfers between devices: none -> 5.91 us  [shards(): other = lax.ppermute(summary, 'tm', [(a, a ^ step) for a in range(blocks)])]
    ppermute x0 -> x3, starting transfers between devices: none -> 5.85 us  [shards(): other = lax.ppermute(summary, 'tm', [(a, a ^ step) for a in range(blocks)])]
    unnamed x10 -> x0, local copies, waits for them, and re-layouts: 4.41 us -> none
    ppermute x3, waiting for transfers between devices: 0.01 us -> 1.63 us  [exchange(): out.append(lax.ppermute(value, axis, [(a, a ^ step) for a in range(count)]))]
    pallas_call x1 -> x3, Pallas kernels: 0.75 us -> 0.8 us  [the longest x1 0.75 us: shards(): pl.pallas_call(functools.partial(finish_kernel, pieces), out_shape=(shape...]
  transfers between devices with their start and end apart: 7 -> 9, of which waited for: 3 -> 6; matrix products, arithmetic and copies ran while one was open for 0% -> 0% of each run, Pallas kernels for 7% -> 9%
where the time goes in v1:
time: 27.5 us; the launch traced here: 27.3 us
  waiting for transfers between devices  11.3 us (41%)
  starting transfers between devices  10.9 us (40%)
  Pallas kernels  3.76 us (14%)
  between operations  0.7 us (3%)
  other arithmetic  0.68 us (2%)
    ppermute x3, waiting for transfers between devices, shards(): other = lax.ppermute(summary, 'tm', [(a, a ^ step) for a in range(blocks)])  5.91 us
    ppermute x3, starting transfers between devices, shards(): other = lax.ppermute(summary, 'tm', [(a, a ^ step) for a in range(blocks)])  5.85 us
    ppermute x3, waiting for transfers between devices, shards(): lax.ppermute(parts[step], 'mode', [(a, a ^ step) for a in range(pieces)])  3.74 us
    ppermute x3, starting transfers between devices, exchange(): out.append(lax.ppermute(value, axis, [(a, a ^ step) for a in range(count)]))  3.08 us
    pallas_call x1, Pallas kernels, shards(): pl.pallas_call(functools.partial(coefficients_kernel, blocks), out_shape=...  2.16 us
    ppermute x3, starting transfers between devices, shards(): lax.ppermute(parts[step], 'mode', [(a, a ^ step) for a in range(pieces)])  1.93 us
    ppermute x3, waiting for transfers between devices, exchange(): out.append(lax.ppermute(value, axis, [(a, a ^ step) for a in range(count)]))  1.63 us
    pallas_call x1, Pallas kernels, shards(): pl.pallas_call(functools.partial(finish_kernel, pieces), out_shape=(shape...  0.75 us
  transfers between devices with their start and end apart: 9, of which 6 were waited for; matrix products, arithmetic and copies ran while one was open for 0% of the time, Pallas kernels for 9%

profile of v1, /device:TPU:0, one launch (start us, length us, event | category | flops | bytes accessed | tf_op | source)
XLA Modules:
  0.0 27.3 jit_solution(2329676780549231033)
XLA Ops:
  0.0 0.5 %collective-permute-start = (bf16[64,512]{1,0:T(8,128)(2,1)}, bf16[64,512]{1,0:T(8,128)(2,1)S(1)}, u32[]{:S(2)}, u32[]{:S(2)}) collective-permute-start(bf16[64,512]{1,0:T(8,128)(2,1)} %refs_2_.1), channel_id=1, source_target_pairs={{0,1},{1,0},{2,3},{3,2},{4,5},{5,4},{6,7},{7,6},{8,9},{9,8},{10,11... | collective-permute-start | bytes 196616 | tf_op jit(solution)/shard_map/ppermute | solution.py:345
  0.5 2.6 %collective-permute-start.2 = (bf16[64,512]{1,0:T(8,128)(2,1)}, bf16[64,512]{1,0:T(8,128)(2,1)S(1)}, u32[]{:S(2)}, u32[]{:S(2)}) collective-permute-start(bf16[64,512]{1,0:T(8,128)(2,1)} %refs_2_.1), channel_id=1, source_target_pairs={{0,3},{1,2},{2,1},{3,0},{4,7},{5,6},{6,5},{7,4},{8,11},{9,10},{10,... | collective-permute-start | bytes 196616 | tf_op jit(solution)/shard_map/ppermute | solution.py:345
  3.1 0.0 collective-permute-start.1
  3.7 2.2 %coefficients.1 = (f32[20,8,512]{2,1,0:T(8,128)S(1)}, f32[4,64,512]{2,1,0:T(8,128)S(1)}, f32[4,16,512]{2,1,0:T(8,128)S(1)}, f32[24,512]{1,0:T(8,128)S(1)}, bf16[...) custom-call(s32[1]{0:T(128)} %bitcast.1.me_ref, f32[1]{0:T(128)S(6)} %copy.6.noise_ref, f32[1,512]{1,0:T(1,128)} %bitcast.4, ...), custom_call_target="tpu_custom_call" | custom-call | flops 20000000 | bytes 2000000 | tf_op jit(solution)/shard_map/coefficients/pallas_call | solution.py:364
  5.9 0.0 collective-permute-done.refs_1_
  5.9 0.0 collective-permute-done.2.refs_3_
  5.9 1.6 %collective-permute-done.1.refs_2_ = bf16[64,512]{1,0:T(8,128)(2,1)S(1)} collective-permute-done((bf16[64,512]{1,0:T(8,128)(2,1)}, bf16[64,512]{1,0:T(8,128)(2,1)S(1)}, u32[]{:S(2)}, u32[]{:S(2)}) %collective-permute-start.1) | collective-permute-done | bytes 65568 | tf_op jit(solution)/shard_map/ppermute | solution.py:345
  7.6 0.5 %rotate.1 = (f32[64,512]{1,0:T(8,128)S(1)}, f32[4,512]{1,0:T(4,128)S(1)}) custom-call(s32[1]{0:T(128)} %bitcast.place_ref, bf16[64,512]{1,0:T(8,128)(2,1)S(1)} %get-tuple-element.17.refs_0_, bf16[64,512]{1,0:T(8,128)(2,1)S(1)} %collective-permute-done.refs_1_, bf16[64,512]{1,0:T(8,128)(2,1)S(1)} %collective-permute-done.1.refs_2_, ...), custom_call_target="tpu_custom_call" | custom-call | tf_op jit(solution)/shard_map/rotate/pallas_call | solution.py:397
  8.1 1.6 %collective-permute-start.3 = (f32[4,512]{1,0:T(4,128)S(1)}, f32[4,512]{1,0:T(4,128)S(1)}, u32[]{:S(2)}, u32[]{:S(2)}) collective-permute-start(f32[4,512]{1,0:T(4,128)S(1)} %get-tuple-element.23.own_ref.refs_0_), channel_id=1, source_target_pairs={{0,4},{4,0},{8,12},{12,8},{16,20},{20,16},{24,28},{28,24},{1,5},{5... | collective-permute-start | bytes 24584 | tf_op jit(solution)/shard_map/ppermute | solution.py:408
  9.6 2.2 %collective-permute-done.3.other_ref.refs_1_ = f32[4,512]{1,0:T(4,128)S(1)} collective-permute-done((f32[4,512]{1,0:T(4,128)S(1)}, f32[4,512]{1,0:T(4,128)S(1)}, u32[]{:S(2)}, u32[]{:S(2)}) %collective-permute-start.3) | collective-permute-done | bytes 8224 | tf_op jit(solution)/shard_map/ppermute | solution.py:408
  11.8 1.6 %collective-permute-start.4 = (f32[4,512]{1,0:T(4,128)S(1)}, f32[4,512]{1,0:T(4,128)S(1)}, u32[]{:S(2)}, u32[]{:S(2)}) collective-permute-start(f32[4,512]{1,0:T(4,128)S(1)} %merge.2.own_ref), channel_id=1, source_target_pairs={{0,8},{4,12},{8,0},{12,4},{16,24},{20,28},{24,16},{28,20},{1,9},{5... | collective-permute-start | bytes 24584 | tf_op jit(solution)/shard_map/ppermute | solution.py:408
  13.5 2.1 %collective-permute-done.4.other_ref.refs_2_ = f32[4,512]{1,0:T(4,128)S(1)} collective-permute-done((f32[4,512]{1,0:T(4,128)S(1)}, f32[4,512]{1,0:T(4,128)S(1)}, u32[]{:S(2)}, u32[]{:S(2)}) %collective-permute-start.4) | collective-permute-done | bytes 8224 | tf_op jit(solution)/shard_map/ppermute | solution.py:408
  15.6 2.7 %collective-permute-start.5 = (f32[4,512]{1,0:T(4,128)S(1)}, f32[4,512]{1,0:T(4,128)S(1)}, u32[]{:S(2)}, u32[]{:S(2)}) collective-permute-start(f32[4,512]{1,0:T(4,128)S(1)} %merge.3), channel_id=1, source_target_pairs={{0,16},{4,20},{8,24},{12,28},{16,0},{20,4},{24,8},{28,12},{1,17},{... | collective-permute-start | bytes 24584 | tf_op jit(solution)/shard_map/ppermute | solution.py:408
  18.2 0.3 %local.1.r_ref = f32[64,512]{1,0:T(8,128)S(1)} custom-call(f32[64,512]{1,0:T(8,128)S(1)} %get-tuple-element.20.z_ref, f32[20,8,512]{2,1,0:T(8,128)S(1)} %get-tuple-element.21.const_ref), custom_call_target="tpu_custom_call" | custom-call | flops 10000000 | bytes 1000000 | tf_op jit(solution)/shard_map/local/pallas_call | solution.py:419
  18.5 1.7 %collective-permute-done.5.refs_3_ = f32[4,512]{1,0:T(4,128)S(1)} collective-permute-done((f32[4,512]{1,0:T(4,128)S(1)}, f32[4,512]{1,0:T(4,128)S(1)}, u32[]{:S(2)}, u32[]{:S(2)}) %collective-permute-start.5) | collective-permute-done | bytes 8224 | tf_op jit(solution)/shard_map/ppermute | solution.py:408
  20.2 0.8 %finish.1 = (f32[64,512]{1,0:T(8,128)S(1)}, bf16[64,512]{1,0:T(8,128)(2,1)S(1)}, bf16[64,512]{1,0:T(8,128)(2,1)S(1)}, bf16[64,512]{1,0:T(8,128)(2,1)S(1)}) custom-call(s32[1]{0:T(128)} %bitcast.place_ref, f32[64,512]{1,0:T(8,128)S(1)} %local.1.r_ref, f32[4,64,512]{2,1,0:T(8,128)S(1)} %get-tuple-element.19.refs_5_.w_ref, ...), custom_call_target="tpu_custom_call" | custom-call | tf_op jit(solution)/shard_map/finish/pallas_call | solution.py:429
  20.9 0.1 collective-permute-start.6
  21.0 1.5 %collective-permute-start.7 = (bf16[64,512]{1,0:T(8,128)(2,1)S(1)}, bf16[64,512]{1,0:T(8,128)(2,1)S(1)}, u32[]{:S(2)}, u32[]{:S(2)}) collective-permute-start(bf16[64,512]{1,0:T(8,128)(2,1)S(1)} %get-tuple-element.27), channel_id=1, source_target_pairs={{0,2},{1,3},{2,0},{3,1},{4,6},{5,7},{6,4},{7,5},{8,10},{9,11},{10,... | collective-permute-start | bytes 196616 | tf_op jit(solution)/shard_map/ppermute | solution.py:440
  22.5 0.4 %collective-permute-start.8 = (bf16[64,512]{1,0:T(8,128)(2,1)S(1)}, bf16[64,512]{1,0:T(8,128)(2,1)S(1)}, u32[]{:S(2)}, u32[]{:S(2)}) collective-permute-start(bf16[64,512]{1,0:T(8,128)(2,1)S(1)} %get-tuple-element.28), channel_id=1, source_target_pairs={{0,3},{1,2},{2,1},{3,0},{4,7},{5,6},{6,5},{7,4},{8,11},{9,10},{10,... | collective-permute-start | bytes 196616 | tf_op jit(solution)/shard_map/ppermute | solution.py:440
  22.9 0.0 collective-permute-done.6
  22.9 2.7 %collective-permute-done.7 = bf16[64,512]{1,0:T(8,128)(2,1)S(1)} collective-permute-done((bf16[64,512]{1,0:T(8,128)(2,1)S(1)}, bf16[64,512]{1,0:T(8,128)(2,1)S(1)}, u32[]{:S(2)}, u32[]{:S(2)}) %collective-permute-start.7) | collective-permute-done | bytes 65568 | tf_op jit(solution)/shard_map/ppermute | solution.py:440
  25.6 1.0 %collective-permute-done.8 = bf16[64,512]{1,0:T(8,128)(2,1)S(1)} collective-permute-done((bf16[64,512]{1,0:T(8,128)(2,1)S(1)}, bf16[64,512]{1,0:T(8,128)(2,1)S(1)}, u32[]{:S(2)}, u32[]{:S(2)}) %collective-permute-start.8) | collective-permute-done | bytes 65568 | tf_op jit(solution)/shard_map/ppermute | solution.py:440
  26.6 0.7 %convert_add_fusion = f32[64,512]{1,0:T(8,128)} fusion(bf16[64,512]{1,0:T(8,128)(2,1)S(1)} %collective-permute-done.8, bf16[64,512]{1,0:T(8,128)(2,1)S(1)} %collective-permute-done.7, f32[64,512]{1,0:T(8,128)S(1)} %get-tuple-element.25, bf16[64,512]{1,0:T(8,128)(2,1)S(1)} %collective-permute-done.6), kind=kLoop, calls=%fused_computation | loop fusion | flops 196608 | bytes 458752 | tf_op jit(solution)/shard_map/add | solution.py:440
  (2 shorter events, 0.1 us)
Async XLA Ops:
  0.0 5.9 %collective-permute-start = (bf16[64,512]{1,0:T(8,128)(2,1)}, bf16[64,512]{1,0:T(8,128)(2,1)S(1)}, u32[]{:S(2)}, u32[]{:S(2)}) collective-permute-start(bf16[64,512]{1,0:T(8,128)(2,1)} %refs_2_.1), channel_id=1, source_target_pairs={{0,1},{1,0},{2,3},{3,2},{4,5},{5,4},{6,7},{7,6},{8,9},{9,8},{10,11... | collective-permute-start | bytes 196616 | tf_op jit(solution)/shard_map/ppermute | solution.py:345
  0.5 5.5 %collective-permute-start.2 = (bf16[64,512]{1,0:T(8,128)(2,1)}, bf16[64,512]{1,0:T(8,128)(2,1)S(1)}, u32[]{:S(2)}, u32[]{:S(2)}) collective-permute-start(bf16[64,512]{1,0:T(8,128)(2,1)} %refs_2_.1), channel_id=1, source_target_pairs={{0,3},{1,2},{2,1},{3,0},{4,7},{5,6},{6,5},{7,4},{8,11},{9,10},{10,... | collective-permute-start | bytes 196616 | tf_op jit(solution)/shard_map/ppermute | solution.py:345
  3.1 4.5 %collective-permute-start.1 = (bf16[64,512]{1,0:T(8,128)(2,1)}, bf16[64,512]{1,0:T(8,128)(2,1)S(1)}, u32[]{:S(2)}, u32[]{:S(2)}) collective-permute-start(bf16[64,512]{1,0:T(8,128)(2,1)} %refs_2_.1), channel_id=1, source_target_pairs={{0,2},{1,3},{2,0},{3,1},{4,6},{5,7},{6,4},{7,5},{8,10},{9,11},{10,... | collective-permute-start | bytes 196616 | tf_op jit(solution)/shard_map/ppermute | solution.py:345
  8.1 3.7 %collective-permute-start.3 = (f32[4,512]{1,0:T(4,128)S(1)}, f32[4,512]{1,0:T(4,128)S(1)}, u32[]{:S(2)}, u32[]{:S(2)}) collective-permute-start(f32[4,512]{1,0:T(4,128)S(1)} %get-tuple-element.23.own_ref.refs_0_), channel_id=1, source_target_pairs={{0,4},{4,0},{8,12},{12,8},{16,20},{20,16},{24,28},{28,24},{1,5},{5... | collective-permute-start | bytes 24584 | tf_op jit(solution)/shard_map/ppermute | solution.py:408
  11.8 3.7 %collective-permute-start.4 = (f32[4,512]{1,0:T(4,128)S(1)}, f32[4,512]{1,0:T(4,128)S(1)}, u32[]{:S(2)}, u32[]{:S(2)}) collective-permute-start(f32[4,512]{1,0:T(4,128)S(1)} %merge.2.own_ref), channel_id=1, source_target_pairs={{0,8},{4,12},{8,0},{12,4},{16,24},{20,28},{24,16},{28,20},{1,9},{5... | collective-permute-start | bytes 24584 | tf_op jit(solution)/shard_map/ppermute | solution.py:408
  15.6 4.6 %collective-permute-start.5 = (f32[4,512]{1,0:T(4,128)S(1)}, f32[4,512]{1,0:T(4,128)S(1)}, u32[]{:S(2)}, u32[]{:S(2)}) collective-permute-start(f32[4,512]{1,0:T(4,128)S(1)} %merge.3), channel_id=1, source_target_pairs={{0,16},{4,20},{8,24},{12,28},{16,0},{20,4},{24,8},{28,12},{1,17},{... | collective-permute-start | bytes 24584 | tf_op jit(solution)/shard_map/ppermute | solution.py:408
  20.9 1.9 %collective-permute-start.6 = (bf16[64,512]{1,0:T(8,128)(2,1)S(1)}, bf16[64,512]{1,0:T(8,128)(2,1)S(1)}, u32[]{:S(2)}, u32[]{:S(2)}) collective-permute-start(bf16[64,512]{1,0:T(8,128)(2,1)S(1)} %get-tuple-element.26), channel_id=1, source_target_pairs={{0,1},{1,0},{2,3},{3,2},{4,5},{5,4},{6,7},{7,6},{8,9},{9,8},{10,11... | collective-permute-start | bytes 196616 | tf_op jit(solution)/shard_map/ppermute | solution.py:440
  21.0 4.6 %collective-permute-start.7 = (bf16[64,512]{1,0:T(8,128)(2,1)S(1)}, bf16[64,512]{1,0:T(8,128)(2,1)S(1)}, u32[]{:S(2)}, u32[]{:S(2)}) collective-permute-start(bf16[64,512]{1,0:T(8,128)(2,1)S(1)} %get-tuple-element.27), channel_id=1, source_target_pairs={{0,2},{1,3},{2,0},{3,1},{4,6},{5,7},{6,4},{7,5},{8,10},{9,11},{10,... | collective-permute-start | bytes 196616 | tf_op jit(solution)/shard_map/ppermute | solution.py:440
  22.5 4.1 %collective-permute-start.8 = (bf16[64,512]{1,0:T(8,128)(2,1)S(1)}, bf16[64,512]{1,0:T(8,128)(2,1)S(1)}, u32[]{:S(2)}, u32[]{:S(2)}) collective-permute-start(bf16[64,512]{1,0:T(8,128)(2,1)S(1)} %get-tuple-element.28), channel_id=1, source_target_pairs={{0,3},{1,2},{2,1},{3,0},{4,7},{5,6},{6,5},{7,4},{8,11},{9,10},{10,... | collective-permute-start | bytes 196616 | tf_op jit(solution)/shard_map/ppermute | solution.py:440
